TPU v7x, 32 devices: a whole 2x2x4 slice. The times are simulated.
32 devices in a mesh: parts: 2 (over y), tm: 4 (over z), chan: 2 (over x), sub: 2 (over core).
Axes of the slice: x: 2, y: 2, z: 4, core: 2. Of those that a mesh axis runs over, the one named last changes fastest.
Arguments:
- start_state: float32 [16, 2048], P(('parts', 'chan')), parts along dimension 0, may hold values from -6 to 6
- guess: bfloat16 [64, 8, 2048], P(('parts', 'tm', 'sub'), 'chan'), parts along dimension 0, may hold values from -6 to 6
- w_in: bfloat16 [576, 320], replicated, may hold values from -0.25 to 0.25
- w_mid: bfloat16 [2880, 320], replicated, may hold values from -0.109375 to 0.109375
- w_out: bfloat16 [2880, 64], replicated, may hold values from -0.875 to 0.875
- time_embed: bfloat16 [1000, 320], replicated, may hold values from -4 to 4
- levels: float32 [1000], replicated, may hold values from 0 to 70, as said below
- plan: int32 [130], P('parts'), parts along dimension 0, may hold values from 0 to 999, as said below
- offset: int32 [2], P('parts'), parts along dimension 0, may hold values from 0 to 32
Outputs:
- trajectory: float32 [64, 8, 2048], P(('parts', 'tm', 'sub'), 'chan'), parts along dimension 0
There are 2 independent parts, one for each index of `parts`. A program takes and returns all parts, laid end to end along the dimension named above; an argument that names none is the same for every part. Nothing has to cross between parts.
Inputs may be any that keep to these rules, and one draw needn't show every extreme that they name: `levels`: rises strictly with the timestep, by at most 0.07 from one timestep to the next. Strictly falling along the plan; the first entry is 999 and the last is 0.
All inputs are finite; a program needn't handle non-finite values.
Results may differ from a plain program's by a relative error of at most 0.003.
Values may be sent and summed in bfloat16 or wider, within the bound.
A program may use at most 64 MiB of HBM per device.

v0:
```python
import jax
import jax.numpy as jnp
from jax import lax
from jax.sharding import PartitionSpec as P

ITERS = 2


def padded_2(block, sides, width):
    for axis, dim in sides:
        count = lax.axis_size(axis)
        forward = [(i, i + 1) for i in range(count - 1)]
        backward = [(target, source) for source, target in forward]
        low = lax.ppermute(
            lax.slice_in_dim(block, block.shape[dim] - width, None, axis=dim), axis, forward
        )
        high = lax.ppermute(lax.slice_in_dim(block, 0, width, axis=dim), axis, backward)
        block = jnp.concatenate([low, block, high], axis=dim)
    return block


def from_behind(array, axis, by):
    devices = lax.axis_size(axis)
    pairs = [(i, i + by) for i in range(devices) if 0 <= i + by < devices]
    return lax.ppermute(array, axis, pairs)


def carried_in(array, axis, combine, identity):
    devices, mine = (lax.axis_size(axis), lax.axis_index(axis))
    everything = lax.all_gather(array, axis)
    start = jnp.broadcast_to(jnp.asarray(identity, array.dtype), array.shape)

    def turn(k, before):
        reached = k < mine
        new = combine(before, everything[k])
        return jnp.where(reached, new, before)

    return lax.fori_loop(0, devices, turn, start)


def conv_valid(layer_in, weight):
    batch_size, rows_in, width_in, channels = layer_in.shape
    padded = jnp.pad(layer_in, ((0, 0), (0, 0), (1, 1), (0, 0)))
    rows_out = rows_in - 2
    patches = jnp.concatenate(
        [
            padded[:, row_off : row_off + rows_out, col_off : col_off + width_in, :]
            for row_off in range(3)
            for col_off in range(3)
        ],
        axis=-1,
    )
    product = jnp.dot(patches.reshape(-1, 9 * channels), weight, preferred_element_type=jnp.float32)
    return product.reshape(batch_size, rows_out, width_in, weight.shape[1])


def row_mask(values, first_row, total_rows):
    positions = first_row + jnp.arange(values.shape[1], dtype=jnp.int32)
    inside = (positions >= 0) & (positions < total_rows)
    return jnp.where(inside[None, :, None, None], values, 0.0)


def drift(layer_in, embed, w_in, w_mid, w_out):
    steps_dev, tile_rows, merged = layer_in.shape
    channels = w_out.shape[1]
    columns = merged // channels
    rimmed = padded_2(layer_in, (("chan", 1),), 3)
    first_row = lax.axis_index("chan") * tile_rows - 2
    total_rows = tile_rows * lax.axis_size("chan")
    first_act = (
        conv_valid(rimmed.reshape(steps_dev, tile_rows + 6, columns, channels), w_in)
        + embed[:, None, None, :]
    )
    first_hidden = row_mask(jax.nn.silu(first_act), first_row, total_rows).astype(jnp.bfloat16)
    second_act = jax.nn.silu(conv_valid(first_hidden, w_mid))
    second_hidden = row_mask(second_act, first_row + 1, total_rows).astype(jnp.bfloat16)
    drift_out = conv_valid(second_hidden, w_out)
    return drift_out.reshape(steps_dev, tile_rows, merged)


def shards(start_state, guess, w_in, w_mid, w_out, time_embed, levels, plan, offset):
    steps_dev = guess.shape[0]
    time_index = lax.axis_index(("tm", "sub"))
    first_step = time_index * steps_dev
    window_ids = lax.dynamic_slice_in_dim(plan, offset[0] + first_step, steps_dev + 1)
    one_hot = window_ids[:, None] == jnp.arange(levels.shape[0], dtype=jnp.int32)[None, :]
    noise = jnp.dot(one_hot.astype(jnp.float32), levels, precision=lax.Precision.HIGHEST)
    step_size = noise[1:] - noise[:-1]
    embed = jnp.dot(
        one_hot[:-1].astype(jnp.bfloat16), time_embed, preferred_element_type=jnp.float32
    )
    factor = jnp.where(first_step + jnp.arange(steps_dev, dtype=jnp.int32) == 0, 1.0, 1.5).astype(
        jnp.float32
    )
    layer_in = guess
    states_after = None
    for sweep in range(ITERS):
        drift_now = drift(layer_in, embed, w_in, w_mid, w_out)
        previous = from_behind(drift_now[-1], ("tm", "sub"), 1)
        earlier = jnp.concatenate([previous[None], drift_now[:-1]], axis=0)
        increment = step_size[:, None, None] * (factor[:, None, None] * drift_now - 0.5 * earlier)
        running = jnp.cumsum(increment, axis=0)
        device_total = running[-1]
        earlier_sum = carried_in(
            device_total,
            ("tm", "sub"),
            lambda before_sum, later_sum: before_sum + later_sum,
            jnp.zeros_like(device_total),
        )
        base_state = start_state + earlier_sum
        states_after = base_state[None] + running
        states_before = states_after - increment
        layer_in = states_before.astype(jnp.bfloat16)
    return states_after


def solution(mesh):
    return jax.shard_map(
        shards,
        mesh=mesh,
        in_specs=(
            P(("parts", "chan"), None),
            P(("parts", "tm", "sub"), "chan", None),
            P(),
            P(),
            P(),
            P(),
            P(),
            P("parts"),
            P("parts"),
        ),
        out_specs=P(("parts", "tm", "sub"), "chan", None),
        check_vma=False,
    )
```

profile of v0, /device:TPU:0, one launch (start us, length us, event | category | flops | bytes accessed | tf_op | source)
XLA Modules:
  0.0 128.7 jit_solution(10329179195908756646)
XLA Ops:
  0.0 0.0 copy-start
  0.0 1.1 fusion.27
  1.1 4.8 %collective-permute-start = (bf16[4,3,2048]{2,1,0:T(4,128)(2,1)S(1)}, bf16[4,3,2048]{2,1,0:T(4,128)(2,1)S(1)}, u32[]{:S(2)}, u32[]{:S(2)}) collective-permute-start(bf16[4,3,2048]{2,1,0:T(4,128)(2,1)S(1)} %get-tuple-element.267), channel_id=1, source_target_pairs={{0,2},{1,3},{4,6},{5,7},{8,10},{9,11},{12,14},{13,15},{16,18},{17,... | collective-permute-start | bytes 147464 | tf_op jit(solution)/shard_map/ppermute | solution.py:14
  5.9 1.3 %collective-permute-start.1 = (bf16[4,3,2048]{2,1,0:T(4,128)(2,1)S(1)}, bf16[4,3,2048]{2,1,0:T(4,128)(2,1)S(1)}, u32[]{:S(2)}, u32[]{:S(2)}) collective-permute-start(bf16[4,3,2048]{2,1,0:T(4,128)(2,1)S(1)} %get-tuple-element.268), channel_id=1, source_target_pairs={{2,0},{3,1},{6,4},{7,5},{10,8},{11,9},{14,12},{15,13},{18,16},{19,... | collective-permute-start | bytes 147464 | tf_op jit(solution)/shard_map/ppermute | solution.py:17
  7.9 0.7 dynamic_slice.17
  8.6 0.1 iota_compare_fusion
  8.7 0.9 convolution_bitcast_fusion
  9.6 1.4 %fusion.22 = f32[4,320]{1,0:T(4,128)S(1)} fusion(bf16[1000,320]{0,1:T(8,128)(2,1)} %param.18, pred[5,1000]{1,0:T(8,128)(4,1)S(1)} %iota_compare_fusion), kind=kOutput, calls=%fused_computation.67 | convolution fusion | flops 2560000 | bytes 649216 | tf_op jit(solution)/shard_map/dot_general | solution.py:89
  11.0 0.0 collective-permute-done
  11.0 1.1 collective-permute-done.1
  12.1 1.0 pad_maximum_fusion
  13.1 0.3 reshape.67
  13.4 1.5 %pad_slice_fusion.30 = (bf16[4,8,32,64]{3,2,1,0:T(8,128)(2,1)S(1)}, bf16[4,8,32,64]{3,2,1,0:T(8,128)(2,1)}, bf16[4,8,32,64]{3,2,1,0:T(8,128)(2,1)}, bf16[4,8,32,...) fusion(bf16[4,10,32,64]{3,2,1,0:T(8,128)(2,1)S(1)} %reshape.67), kind=kLoop, calls=%fused_computation.43 | loop fusion | bytes 2293760 | tf_op jit(solution)/shard_map/slice | solution.py:47
  14.9 2.7 %concatenate.31 = bf16[4,8,32,576]{3,2,1,0:T(8,128)(2,1)S(1)} concatenate(bf16[4,8,32,64]{3,2,1,0:T(8,128)(2,1)} %get-tuple-element.263, bf16[4,8,32,64]{3,2,1,0:T(8,128)(2,1)} %get-tuple-element.262, bf16[4,8,32,64]{3,2,1,0:T(8,128)(2,1)} %get-tuple-element.257, bf16[4,8,32,64]{3,2,1,0:T(8,128)(2,1)} %get-tuple-element.258, bf16[4,8,32,64]{3,2,1,0:T(8,128)(2,1)} %get-tuple-element.261, ...), dimensions={3} | concatenate | bytes 2359296 | tf_op jit(solution)/shard_map/concatenate | solution.py:45
  17.6 2.1 %select_convert_fusion.1 = bf16[4,8,32,320]{3,2,1,0:T(8,128)(2,1)S(1)} fusion(bf16[4,8,32,576]{3,2,1,0:T(8,128)(2,1)S(1)} %concatenate.31, f32[4,320]{1,0:T(4,128)S(1)} %fusion.22, pred[8]{0:T(512)(128)(4,1)S(1)} %compare_and_fusion, bf16[576,320]{0,1:T(8,128)(2,1)} %param.15), kind=kOutput, calls=%fused_computation.7 | convolution fusion | flops 379781120 | bytes 2208776 | tf_op jit(solution)/shard_map/dot_general | solution.py:53
  19.7 2.4 %pad_slice_fusion.6 = (bf16[4,6,32,320]{3,2,1,0:T(8,128)(2,1)S(1)}, bf16[4,6,32,320]{3,2,1,0:T(8,128)(2,1)S(1)}, bf16[4,6,32,320]{3,2,1,0:T(8,128)(2,1)}, bf16[4...) fusion(bf16[4,8,32,320]{3,2,1,0:T(8,128)(2,1)S(1)} %select_conv, ...), kind=kLoop, calls=%fused_computation.17 | loop fusion | bytes 6979584 | tf_op jit(solution)/shard_map/slice | solution.py:47
  22.2 8.1 %concatenate.32 = bf16[4,6,32,2880]{3,2,1,0:T(8,128)(2,1)} concatenate(bf16[4,6,32,320]{3,2,1,0:T(8,128)(2,1)} %get-tuple-element.228, bf16[4,6,32,320]{3,2,1,0:T(8,128)(2,1)} %get-tuple-element.227, bf16[4,6,32,320]{3,2,1,0:T(8,128)(2,1)S(1)} %get-tuple-element.221, bf16[4,6,32,320]{3,2,1,0:T(8,128)(2,1)} %get-tuple-element.222, bf16[4,6,32,320]{3,2,1,0:T(8,128)(2,1)} %get-tuple-element.226, ...), dimensions={3} | concatenate | bytes 8847360 | tf_op jit(solution)/shard_map/concatenate | solution.py:45
  30.3 0.0 copy-done
  30.3 4.9 %select_convert_fusion.3 = bf16[4,6,32,320]{3,2,1,0:T(8,128)(2,1)S(1)} fusion(bf16[4,6,32,2880]{3,2,1,0:T(8,128)(2,1)} %concatenate.32, bf16[2880,320]{0,1:T(8,128)(2,1)S(1)} %copy-done, pred[6]{0:T(512)(128)(4,1)S(1)} %compare_and_fusion.1), kind=kOutput, calls=%fused_computation.9 | convolution fusion | flops 1417052160 | bytes 6758406 | tf_op jit(solution)/shard_map/dot_general | solution.py:53
  35.2 1.5 %pad_slice_fusion.18 = (bf16[4,4,32,320]{3,2,1,0:T(8,128)(2,1)S(1)}, bf16[4,4,32,320]{3,2,1,0:T(8,128)(2,1)S(1)}, bf16[4,4,32,320]{3,2,1,0:T(8,128)(2,1)S(1)}, b...) fusion(bf16[4,6,32,320]{3,2,1,0:T(8,128)(2,1)S(1)} %select_conv, ...), kind=kLoop, calls=%fused_computation.29 | loop fusion | bytes 4718592 | tf_op jit(solution)/shard_map/slice | solution.py:47
  36.8 5.8 %concatenate.33 = bf16[4,4,32,2880]{3,2,1,0:T(8,128)(2,1)} concatenate(bf16[4,4,32,320]{3,2,1,0:T(8,128)(2,1)} %get-tuple-element.246, bf16[4,4,32,320]{3,2,1,0:T(8,128)(2,1)} %get-tuple-element.245, bf16[4,4,32,320]{3,2,1,0:T(8,128)(2,1)S(1)} %get-tuple-element.239, bf16[4,4,32,320]{3,2,1,0:T(8,128)(2,1)S(1)} %get-tuple-element.240, bf16[4,4,32,320]{3,2,1,0:T(8,128)(2,1)} %get-tuple-element.244, ...), dimensions={3} | concatenate | bytes 5898240 | tf_op jit(solution)/shard_map/concatenate | solution.py:45
  42.5 2.9 %fusion.29 = f32[512,64]{0,1:T(8,128)S(1)} fusion(bf16[512,2880]{1,0:T(8,128)(2,1)} %bitcast.49, bf16[2880,64]{0,1:T(8,128)(2,1)} %param.17), kind=kOutput, calls=%fused_computation.78 | convolution fusion | flops 188743680 | bytes 3448832 | tf_op jit(solution)/shard_map/dot_general | solution.py:53
  45.5 0.1 copy.32
  45.6 0.1 squeeze.24
  45.6 1.3 %collective-permute-start.2 = (f32[4,2048]{1,0:T(4,128)S(1)}, f32[4,2048]{1,0:T(4,128)S(1)}, u32[]{:S(2)}, u32[]{:S(2)}) collective-permute-start(f32[4,2048]{1,0:T(4,128)S(1)} %squeeze.24), channel_id=1, source_target_pairs={{0,1},{1,4},{4,5},{5,8},{8,9},{9,12},{12,13},{2,3},{3,6},{6,7},{7,... | collective-permute-start | bytes 98312 | tf_op jit(solution)/shard_map/ppermute | solution.py:25
  46.9 0.1 compare_select_fusion
  47.0 0.0 copy-start.1
  47.0 0.1 copy.31
  47.2 0.1 reshape_reshape.6
  47.3 0.1 copy.33
  47.4 0.1 slice.261
  47.6 0.2 collective-permute-done.2
  47.8 0.1 fusion.11
  47.9 17.5 %all_gather.6 = f32[8,4,2048]{2,1,0:T(4,128)S(1)} all-gather(f32[1,4,2048]{2,1,0:T(4,128)S(1)} %slice.308), channel_id=1, replica_groups=mesh['parts'=2,'tm'=4,'chan'=2,'sub'=2] {'tm','sub'}, dimensions={0}, use_global_device_ids=true | all-gather | bytes 294912 | tf_op jit(solution)/shard_map/all_gather | solution.py:30
  65.5 0.4 while.28
  65.8 0.0 copy-done.1
  66.0 3.5 %collective-permute-start.3 = (bf16[4,3,2048]{2,1,0:T(4,128)(2,1)S(1)}, bf16[4,3,2048]{2,1,0:T(4,128)(2,1)S(1)}, u32[]{:S(2)}, u32[]{:S(2)}) collective-permute-start(bf16[4,3,2048]{2,1,0:T(4,128)(2,1)S(1)} %get-tuple-element.265), channel_id=1, source_target_pairs={{0,2},{1,3},{4,6},{5,7},{8,10},{9,11},{12,14},{13,15},{16,18},{17,... | collective-permute-start | bytes 147464 | tf_op jit(solution)/shard_map/ppermute | solution.py:14
  69.5 1.5 %collective-permute-start.4 = (bf16[4,3,2048]{2,1,0:T(4,128)(2,1)S(1)}, bf16[4,3,2048]{2,1,0:T(4,128)(2,1)S(1)}, u32[]{:S(2)}, u32[]{:S(2)}) collective-permute-start(bf16[4,3,2048]{2,1,0:T(4,128)(2,1)S(1)} %get-tuple-element.266), channel_id=1, source_target_pairs={{2,0},{3,1},{6,4},{7,5},{10,8},{11,9},{14,12},{15,13},{18,16},{19,... | collective-permute-start | bytes 147464 | tf_op jit(solution)/shard_map/ppermute | solution.py:17
  71.0 0.4 collective-permute-done.3
  71.4 4.3 %collective-permute-done.4 = bf16[4,3,2048]{2,1,0:T(4,128)(2,1)S(1)} collective-permute-done((bf16[4,3,2048]{2,1,0:T(4,128)(2,1)S(1)}, bf16[4,3,2048]{2,1,0:T(4,128)(2,1)S(1)}, u32[]{:S(2)}, u32[]{:S(2)}) %collective-permute-start.4) | collective-permute-done | bytes 49184 | tf_op jit(solution)/shard_map/ppermute | solution.py:17
  75.7 0.2 pad_maximum_fusion.1
  75.8 0.3 reshape.68
  76.1 1.5 %pad_slice_fusion.24 = (bf16[4,8,32,64]{3,2,1,0:T(8,128)(2,1)S(1)}, bf16[4,8,32,64]{3,2,1,0:T(8,128)(2,1)}, bf16[4,8,32,64]{3,2,1,0:T(8,128)(2,1)}, bf16[4,8,32,...) fusion(bf16[4,10,32,64]{3,2,1,0:T(8,128)(2,1)S(1)} %reshape.68), kind=kLoop, calls=%fused_computation.37 | loop fusion | bytes 2293760 | tf_op jit(solution)/shard_map/slice | solution.py:47
  77.6 2.7 %concatenate.36 = bf16[4,8,32,576]{3,2,1,0:T(8,128)(2,1)S(1)} concatenate(bf16[4,8,32,64]{3,2,1,0:T(8,128)(2,1)} %get-tuple-element.254, bf16[4,8,32,64]{3,2,1,0:T(8,128)(2,1)} %get-tuple-element.253, bf16[4,8,32,64]{3,2,1,0:T(8,128)(2,1)} %get-tuple-element.248, bf16[4,8,32,64]{3,2,1,0:T(8,128)(2,1)} %get-tuple-element.249, bf16[4,8,32,64]{3,2,1,0:T(8,128)(2,1)} %get-tuple-element.252, ...), dimensions={3} | concatenate | bytes 2359296 | tf_op jit(solution)/shard_map/concatenate | solution.py:45
  80.4 2.1 %select_convert_fusion = bf16[4,8,32,320]{3,2,1,0:T(8,128)(2,1)S(1)} fusion(bf16[4,8,32,576]{3,2,1,0:T(8,128)(2,1)S(1)} %concatenate.36, f32[4,320]{1,0:T(4,128)S(1)} %fusion.22, pred[8]{0:T(512)(128)(4,1)S(1)} %compare_and_fusion, bf16[576,320]{0,1:T(8,128)(2,1)} %param.15), kind=kOutput, calls=%fused_computation.6 | convolution fusion | flops 379781120 | bytes 2208776 | tf_op jit(solution)/shard_map/dot_general | solution.py:53
  82.5 2.4 %pad_slice_fusion = (bf16[4,6,32,320]{3,2,1,0:T(8,128)(2,1)S(1)}, bf16[4,6,32,320]{3,2,1,0:T(8,128)(2,1)S(1)}, bf16[4,6,32,320]{3,2,1,0:T(8,128)(2,1)}, bf16[4,6...) fusion(bf16[4,8,32,320]{3,2,1,0:T(8,128)(2,1)S(1)} %select_conv, ...), kind=kLoop, calls=%fused_computation.11 | loop fusion | bytes 6979584 | tf_op jit(solution)/shard_map/slice | solution.py:47
  84.9 8.1 %concatenate.37 = bf16[4,6,32,2880]{3,2,1,0:T(8,128)(2,1)} concatenate(bf16[4,6,32,320]{3,2,1,0:T(8,128)(2,1)} %get-tuple-element.219, bf16[4,6,32,320]{3,2,1,0:T(8,128)(2,1)} %get-tuple-element.218, bf16[4,6,32,320]{3,2,1,0:T(8,128)(2,1)S(1)} %get-tuple-element.212, bf16[4,6,32,320]{3,2,1,0:T(8,128)(2,1)} %get-tuple-element.213, bf16[4,6,32,320]{3,2,1,0:T(8,128)(2,1)} %get-tuple-element.217, ...), dimensions={3} | concatenate | bytes 8847360 | tf_op jit(solution)/shard_map/concatenate | solution.py:45
  93.0 4.9 %select_convert_fusion.2 = bf16[4,6,32,320]{3,2,1,0:T(8,128)(2,1)S(1)} fusion(bf16[4,6,32,2880]{3,2,1,0:T(8,128)(2,1)} %concatenate.37, bf16[2880,320]{0,1:T(8,128)(2,1)S(1)} %copy-done, pred[6]{0:T(512)(128)(4,1)S(1)} %compare_and_fusion.1), kind=kOutput, calls=%fused_computation.8 | convolution fusion | flops 1417052160 | bytes 6758406 | tf_op jit(solution)/shard_map/dot_general | solution.py:53
  97.9 1.5 %pad_slice_fusion.12 = (bf16[4,4,32,320]{3,2,1,0:T(8,128)(2,1)S(1)}, bf16[4,4,32,320]{3,2,1,0:T(8,128)(2,1)S(1)}, bf16[4,4,32,320]{3,2,1,0:T(8,128)(2,1)S(1)}, b...) fusion(bf16[4,6,32,320]{3,2,1,0:T(8,128)(2,1)S(1)} %select_conv, ...), kind=kLoop, calls=%fused_computation.23 | loop fusion | bytes 4718592 | tf_op jit(solution)/shard_map/slice | solution.py:47
  99.5 5.8 %concatenate.38 = bf16[4,4,32,2880]{3,2,1,0:T(8,128)(2,1)} concatenate(bf16[4,4,32,320]{3,2,1,0:T(8,128)(2,1)} %get-tuple-element.237, bf16[4,4,32,320]{3,2,1,0:T(8,128)(2,1)} %get-tuple-element.236, bf16[4,4,32,320]{3,2,1,0:T(8,128)(2,1)S(1)} %get-tuple-element.230, bf16[4,4,32,320]{3,2,1,0:T(8,128)(2,1)S(1)} %get-tuple-element.231, bf16[4,4,32,320]{3,2,1,0:T(8,128)(2,1)} %get-tuple-element.235, ...), dimensions={3} | concatenate | bytes 5898240 | tf_op jit(solution)/shard_map/concatenate | solution.py:45
  105.2 2.9 %fusion.30 = f32[512,64]{0,1:T(8,128)S(1)} fusion(bf16[512,2880]{1,0:T(8,128)(2,1)} %bitcast.50, bf16[2880,64]{0,1:T(8,128)(2,1)} %param.17), kind=kOutput, calls=%fused_computation.79 | convolution fusion | flops 188743680 | bytes 3448832 | tf_op jit(solution)/shard_map/dot_general | solution.py:53
  108.2 0.1 copy.40
  108.3 0.1 squeeze.25
  108.4 1.3 %collective-permute-start.5 = (f32[4,2048]{1,0:T(4,128)S(1)}, f32[4,2048]{1,0:T(4,128)S(1)}, u32[]{:S(2)}, u32[]{:S(2)}) collective-permute-start(f32[4,2048]{1,0:T(4,128)S(1)} %squeeze.25), channel_id=1, source_target_pairs={{0,1},{1,4},{4,5},{5,8},{8,9},{9,12},{12,13},{2,3},{3,6},{6,7},{7,... | collective-permute-start | bytes 98312 | tf_op jit(solution)/shard_map/ppermute | solution.py:25
  109.7 0.1 copy.39
  109.8 0.1 reshape_reshape.7
  110.0 0.1 copy.41
  110.1 0.1 slice.294
  110.2 0.3 collective-permute-done.5
  110.5 0.1 fusion.14
  110.6 17.0 %all_gather.7 = f32[8,4,2048]{2,1,0:T(4,128)S(1)} all-gather(f32[1,4,2048]{2,1,0:T(4,128)S(1)} %slice.322), channel_id=1, replica_groups=mesh['parts'=2,'tm'=4,'chan'=2,'sub'=2] {'tm','sub'}, dimensions={0}, use_global_device_ids=true | all-gather | bytes 294912 | tf_op jit(solution)/shard_map/all_gather | solution.py:30
  127.7 0.4 while.29
  128.1 0.7 broadcast_add_fusion
  (32 shorter events, 0.6 us)
Async XLA Ops:
  0.0 30.3 %copy-start = (bf16[2880,320]{0,1:T(8,128)(2,1)S(1)}, bf16[2880,320]{0,1:T(8,128)(2,1)}, u32[]{:S(2)}) copy-start(bf16[2880,320]{0,1:T(8,128)(2,1)} %param.16) | copy-start | bytes 5529604
  1.1 9.9 %collective-permute-start = (bf16[4,3,2048]{2,1,0:T(4,128)(2,1)S(1)}, bf16[4,3,2048]{2,1,0:T(4,128)(2,1)S(1)}, u32[]{:S(2)}, u32[]{:S(2)}) collective-permute-start(bf16[4,3,2048]{2,1,0:T(4,128)(2,1)S(1)} %get-tuple-element.267), channel_id=1, source_target_pairs={{0,2},{1,3},{4,6},{5,7},{8,10},{9,11},{12,14},{13,15},{16,18},{17,... | collective-permute-start | bytes 147464 | tf_op jit(solution)/shard_map/ppermute | solution.py:14
  5.9 6.2 %collective-permute-start.1 = (bf16[4,3,2048]{2,1,0:T(4,128)(2,1)S(1)}, bf16[4,3,2048]{2,1,0:T(4,128)(2,1)S(1)}, u32[]{:S(2)}, u32[]{:S(2)}) collective-permute-start(bf16[4,3,2048]{2,1,0:T(4,128)(2,1)S(1)} %get-tuple-element.268), channel_id=1, source_target_pairs={{2,0},{3,1},{6,4},{7,5},{10,8},{11,9},{14,12},{15,13},{18,16},{19,... | collective-permute-start | bytes 147464 | tf_op jit(solution)/shard_map/ppermute | solution.py:17
  45.6 2.1 %collective-permute-start.2 = (f32[4,2048]{1,0:T(4,128)S(1)}, f32[4,2048]{1,0:T(4,128)S(1)}, u32[]{:S(2)}, u32[]{:S(2)}) collective-permute-start(f32[4,2048]{1,0:T(4,128)S(1)} %squeeze.24), channel_id=1, source_target_pairs={{0,1},{1,4},{4,5},{5,8},{8,9},{9,12},{12,13},{2,3},{3,6},{6,7},{7,... | collective-permute-start | bytes 98312 | tf_op jit(solution)/shard_map/ppermute | solution.py:25
  47.0 18.8 %copy-start.1 = (f32[4,2048]{1,0:T(4,128)S(1)}, f32[4,2048]{1,0:T(4,128)}, u32[]{:S(2)}) copy-start(f32[4,2048]{1,0:T(4,128)} %param.13) | copy-start | bytes 98308
  66.0 5.4 %collective-permute-start.3 = (bf16[4,3,2048]{2,1,0:T(4,128)(2,1)S(1)}, bf16[4,3,2048]{2,1,0:T(4,128)(2,1)S(1)}, u32[]{:S(2)}, u32[]{:S(2)}) collective-permute-start(bf16[4,3,2048]{2,1,0:T(4,128)(2,1)S(1)} %get-tuple-element.265), channel_id=1, source_target_pairs={{0,2},{1,3},{4,6},{5,7},{8,10},{9,11},{12,14},{13,15},{16,18},{17,... | collective-permute-start | bytes 147464 | tf_op jit(solution)/shard_map/ppermute | solution.py:14
  69.5 6.2 %collective-permute-start.4 = (bf16[4,3,2048]{2,1,0:T(4,128)(2,1)S(1)}, bf16[4,3,2048]{2,1,0:T(4,128)(2,1)S(1)}, u32[]{:S(2)}, u32[]{:S(2)}) collective-permute-start(bf16[4,3,2048]{2,1,0:T(4,128)(2,1)S(1)} %get-tuple-element.266), channel_id=1, source_target_pairs={{2,0},{3,1},{6,4},{7,5},{10,8},{11,9},{14,12},{15,13},{18,16},{19,... | collective-permute-start | bytes 147464 | tf_op jit(solution)/shard_map/ppermute | solution.py:17
  108.4 2.1 %collective-permute-start.5 = (f32[4,2048]{1,0:T(4,128)S(1)}, f32[4,2048]{1,0:T(4,128)S(1)}, u32[]{:S(2)}, u32[]{:S(2)}) collective-permute-start(f32[4,2048]{1,0:T(4,128)S(1)} %squeeze.25), channel_id=1, source_target_pairs={{0,1},{1,4},{4,5},{5,8},{8,9},{9,12},{12,13},{2,3},{3,6},{6,7},{7,... | collective-permute-start | bytes 98312 | tf_op jit(solution)/shard_map/ppermute | solution.py:25
where the time goes:
time: 131 us; the launch traced here: 129 us
  local copies, waits for them, and re-layouts  48 us (37%)
  blocking collectives  34.6 us (26%)
  matrix products  22.2 us (17%)
  starting transfers between devices  13.7 us (10%)
  waiting for transfers between devices  6.27 us (5%)
  other arithmetic  2.67 us (2%)
    all_gather x2, blocking collectives, carried_in(): everything = lax.all_gather(array, axis)  34.6 us
    concatenate x6, local copies, waits for them, and re-layouts, conv_valid(): jnp.concatenate([padded[:, row_off:row_off + rows_out, col_off:col_off +...  33.2 us
    dot_general x6, matrix products, conv_valid(): jnp.dot(patches.reshape(-1, 9 * channels), weight, preferred_element_type...  19.9 us
    slice x6, local copies, waits for them, and re-layouts, conv_valid(): padded[:, row_off:row_off + rows_out, col_off:col_off + width_in, :]  10.9 us
    ppermute x2, starting transfers between devices, padded_2(): lax.ppermute(lax.slice_in_dim(block, block.shape[dim] - width, None, axis...  8.35 us
    ppermute x2, waiting for transfers between devices, padded_2(): lax.ppermute(lax.slice_in_dim(block, 0, width, axis=dim), axis, backward)  5.33 us
    ppermute x2, starting transfers between devices, padded_2(): lax.ppermute(lax.slice_in_dim(block, 0, width, axis=dim), axis, backward)  2.76 us
  transfers between devices with their start and end apart: 6, of which 5 were waited for; matrix products, arithmetic and copies ran while one was open for 3% of the time, Pallas kernels for 0%

commit v1 on v0

v1 whole, which is shorter than its diff:
```python
import functools

import jax
import jax.numpy as jnp
from jax import lax
from jax.experimental import pallas as pl
from jax.experimental.pallas import tpu as pltpu
from jax.sharding import PartitionSpec as P

ITERS = 2
MESH = pl.DeviceIdType.MESH
F32 = jnp.float32
BF16 = jnp.bfloat16


def silu(v):
    half = 0.5 * v
    return half + half * jnp.tanh(half)


def fold(array):
    half = array.shape[0] // 2
    return jnp.concatenate([array[:half], array[half:]], axis=1)


def unfold(array):
    half = array.shape[1] // 2
    return jnp.concatenate([array[:, :half], array[:, half:]], axis=0)


def body(
    cfg,
    start_ref, guess_ref, levels_ref, plan_ref, offset_ref, w_in_hbm, w_mid_hbm, w_out_hbm, te_hbm,
    out_ref,
    w_in, w_mid, w_out, te, w_sum, x1, x2, x3, u_scr, st_scr, o_scr, p_scr,
    halo_send, halo_recv, t_send, t_recv, s_send, s_recv, d_send, d_recv,
    w_sem, hs_sem, hr_sem, ts_sem, tr_sem, ss_sem, sr_sem, ds_sem, dr_sem,
):
    steps, rows, cols, ch, hid, n_chan, n_tm, n_levels, n_plan, two = cfg
    block = steps * cols
    z = lax.axis_index("tm")
    sub = lax.axis_index("sub")
    chan = lax.axis_index("chan")
    first = (z * 2 + sub) * steps
    has_low = chan > 0
    has_high = chan < n_chan - 1

    weights = [
        pltpu.make_async_copy(src, dst, w_sem.at[i])
        for i, (src, dst) in enumerate(
            [(w_in_hbm, w_in), (te_hbm, te), (w_mid_hbm, w_mid), (w_out_hbm, w_out)]
        )
    ]
    for copy in weights:
        copy.start()

    barrier = pltpu.get_barrier_semaphore()
    next_z = (sub == 1) & (z < n_tm - 1)
    prev_z = (sub == 0) & (z > 0)

    def hello(dev):
        pl.semaphore_signal(barrier, inc=1, device_id=dev, device_id_type=MESH)

    hello({"sub": 1 - sub})
    for k in range(n_tm):
        @pl.when(k != z)
        def _():
            hello({"tm": k})
    @pl.when(next_z)
    def _():
        hello({"tm": z + 1, "sub": 0})
    @pl.when(prev_z)
    def _():
        hello({"tm": z - 1, "sub": 1})
    @pl.when(has_low)
    def _():
        hello({"chan": chan - 1})
    @pl.when(has_high)
    def _():
        hello({"chan": chan + 1})

    for n in range(steps):
        tile = guess_ref[n].astype(F32)
        for c in range(cols):
            u_scr[pl.ds(n * cols + c, rows, stride=block), :] = tile[:, c * ch:(c + 1) * ch]
    for c in range(cols):
        st_scr[pl.ds(c, rows, stride=cols), :] = start_ref[:, c * ch:(c + 1) * ch]

    own = (1 + 2 * chan) if two else 3
    n_in = rows + 4 if two else rows + 6
    n1, n2 = n_in - 2, (n_in - 3 if two else n_in - 4)
    o1 = (1 - chan) if two else 0
    if two:
        x1[pl.ds(pl.multiple_of(chan * (n_in - 1) * block, block), block), :] = jnp.zeros((block, 3 * ch), BF16)
        x2[pl.ds(pl.multiple_of(chan * n1 * block, block), block), :] = jnp.zeros((block, 3 * hid), BF16)
        x3[pl.ds(pl.multiple_of(chan * n2 * block, block), block), :] = jnp.zeros((block, 3 * hid), BF16)
    else:
        x1[...] = jnp.zeros(x1.shape, BF16)

    pl.semaphore_wait(
        barrier,
        n_tm + next_z.astype(jnp.int32) + prev_z.astype(jnp.int32)
        + has_low.astype(jnp.int32) + has_high.astype(jnp.int32),
    )

    def halo_copy(sweep, side):
        return pltpu.make_async_remote_copy(
            src_ref=halo_send.at[sweep, side], dst_ref=halo_recv.at[sweep, side],
            send_sem=hs_sem.at[sweep, side], recv_sem=hr_sem.at[sweep, side],
            device_id={"chan": chan - 1 + 2 * side}, device_id_type=MESH,
        )

    def t_copy(sweep, target):
        return pltpu.make_async_remote_copy(
            src_ref=t_send.at[sweep], dst_ref=t_recv.at[sweep, z],
            send_sem=ts_sem.at[sweep, target], recv_sem=tr_sem.at[sweep, z],
            device_id={"tm": target}, device_id_type=MESH,
        )

    def t_arrived(sweep, source):
        return pltpu.make_async_remote_copy(
            src_ref=t_send.at[sweep], dst_ref=t_recv.at[sweep, source],
            send_sem=ts_sem.at[sweep, source], recv_sem=tr_sem.at[sweep, source],
            device_id={"tm": source}, device_id_type=MESH,
        )

    def s_copy(sweep):
        return pltpu.make_async_remote_copy(
            src_ref=s_send.at[sweep], dst_ref=s_recv.at[sweep],
            send_sem=ss_sem.at[sweep], recv_sem=sr_sem.at[sweep],
            device_id={"sub": 1 - sub}, device_id_type=MESH,
        )

    def d_copy(dev):
        return pltpu.make_async_remote_copy(
            src_ref=d_send, dst_ref=d_recv, send_sem=ds_sem, recv_sem=dr_sem,
            device_id=dev, device_id_type=MESH,
        )

    edge = 3 * block

    def send_halo(sweep):
        halo_send[sweep, 0] = fold(u_scr[0:edge, :]).astype(BF16)
        halo_send[sweep, 1] = fold(u_scr[rows * block - edge:rows * block, :]).astype(BF16)
        for side, there in ((0, has_low), (1, has_high)):
            @pl.when(there)
            def _():
                halo_copy(sweep, side).start()

    send_halo(0)

    base = offset_ref[0] + first
    ids = [plan_ref[jnp.minimum(base + n, n_plan - 1)] for n in range(steps + 2)]
    noise = [levels_ref[i] for i in ids]
    size = [noise[n + 1] - noise[n] for n in range(steps + 1)]
    front = [size[n] * jnp.where(first + n == 0, 1.0, 1.5) for n in range(steps)]
    onward = [front[n] - 0.5 * size[n + 1] for n in range(steps)]

    col_of = lax.broadcasted_iota(jnp.int32, (block, 1), 0) % cols

    def spread(value):
        left = jnp.where(col_of == 0, 0.0, pltpu.roll(value, 1, 0))
        right = jnp.where(col_of == cols - 1, 0.0, pltpu.roll(value, block - 1, 0))
        return jnp.concatenate([left, value, right], axis=1).astype(BF16)

    def at(row):
        if isinstance(row, int):
            return pl.ds(row * block, block)
        return pl.ds(pl.multiple_of(row * block, block), block)

    def chosen(n_rows, first_row, r):
        position = chan * rows + first_row + r
        return ((position >= 0) & (position < n_chan * rows)).astype(F32)

    def own_rows():
        for r in range(rows):
            x1[at(own + r), :] = spread(u_scr[r * block:(r + 1) * block, :])

    own_rows()
    weights[0].wait()
    weights[1].wait()
    hot = jnp.zeros((8, n_levels), F32)
    row_of = lax.broadcasted_iota(jnp.int32, (8, n_levels), 0)
    id_of = lax.broadcasted_iota(jnp.int32, (8, n_levels), 1)
    for n in range(steps):
        hot = jnp.where((row_of == n) & (id_of == ids[n]), 1.0, hot)
    embed8 = jnp.dot(hot.astype(BF16), te[...], preferred_element_type=F32)
    embed = jnp.concatenate(
        [jnp.broadcast_to(embed8[n:n + 1], (cols, hid)) for n in range(steps)], axis=0
    )

    for sweep in range(ITERS):
        for side, there in ((1, has_low), (0, has_high)):
            @pl.when(there)
            def _():
                halo_copy(sweep, side).wait_recv()
                got = unfold(halo_recv[sweep, side].astype(F32))
                for r in range(3):
                    x1[at(r if side == 1 else own + rows + r), :] = spread(got[r * block:(r + 1) * block])
        act = jnp.dot(x1[0:n1 * block, :], w_in[0:3 * ch, :], preferred_element_type=F32)
        for kr in (1, 2):
            act += jnp.dot(
                x1[kr * block:(kr + n1) * block, :], w_in[kr * 3 * ch:(kr + 1) * 3 * ch, :],
                preferred_element_type=F32,
            )
        for r in range(n1):
            hidden = silu(act[r * block:(r + 1) * block] + embed)
            if not two:
                hidden = hidden * chosen(n1, -2, r)
            x2[at(o1 + r), :] = spread(hidden)
        if sweep == 0:
            weights[2].wait()
        act = jnp.dot(x2[0:n2 * block, :], w_mid[0:3 * hid, :], preferred_element_type=F32)
        for kr in (1, 2):
            act += jnp.dot(
                x2[kr * block:(kr + n2) * block, :], w_mid[kr * 3 * hid:(kr + 1) * 3 * hid, :],
                preferred_element_type=F32,
            )
        for r in range(n2):
            hidden = silu(act[r * block:(r + 1) * block])
            if not two:
                hidden = hidden * chosen(n2, -1, r)
            x3[at(o1 + r), :] = spread(hidden)
        if sweep == 0:
            weights[3].wait()
            for kr in range(3):
                w_sum[:, kr * ch:(kr + 1) * ch] = w_out[kr * 3 * hid:(kr + 1) * 3 * hid, :]
        taps = jnp.dot(x3[...], w_sum[...], preferred_element_type=F32)
        size_out = rows * block
        drift = (
            taps[0:size_out, 0:ch]
            + taps[block:block + size_out, ch:2 * ch]
            + taps[2 * block:2 * block + size_out, 2 * ch:3 * ch]
        ).reshape(rows, steps, cols, ch)

        total = jnp.zeros((rows, cols, ch), F32)
        after = []
        for n in range(steps):
            after.append(total + front[n] * drift[:, n])
            total = total + onward[n] * drift[:, n]
        last = sweep == ITERS - 1
        total = fold(total.reshape(rows * cols, ch))
        t_send[sweep] = total
        for k in range(1, n_tm):
            @pl.when(k > z)
            def _():
                t_copy(sweep, k).start()
        if not last:
            d_send[...] = fold(drift[:, steps - 1].reshape(rows * cols, ch))
            @pl.when(sub == 0)
            def _():
                d_copy({"sub": 1}).start()
            @pl.when(next_z)
            def _():
                d_copy({"tm": z + 1, "sub": 0}).start()
        p_scr[...] = jnp.zeros(p_scr.shape, F32)
        for k in range(n_tm - 1):
            @pl.when(k < z)
            def _():
                t_arrived(sweep, k).wait_recv()
                p_scr[...] += t_recv[sweep, k]
        s_send[sweep] = p_scr[...] + jnp.where(sub == 0, total, 0.0)
        s_copy(sweep).start()
        s_copy(sweep).wait_recv()
        origin = st_scr[...].reshape(rows, cols, ch) + unfold(
            p_scr[...] + s_recv[sweep]
        ).reshape(rows, cols, ch)
        if last:
            for n in range(steps):
                o_scr[n * rows * cols:(n + 1) * rows * cols, :] = (origin + after[n]).reshape(rows * cols, ch)
            for c in range(0, cols, 2):
                out_ref[:, c * ch:(c + 2) * ch] = jnp.concatenate(
                    [o_scr[pl.ds(c + i, steps * rows, stride=cols), :] for i in range(2)], axis=1
                )
        else:
            p_scr[...] = jnp.zeros(p_scr.shape, F32)
            @pl.when((sub == 1) | prev_z)
            def _():
                d_copy({"sub": 1 - sub}).wait_recv()
                p_scr[...] = d_recv[...]
            behind = unfold(p_scr[...]).reshape(rows, cols, ch)
            before = [origin + (0.5 * size[0]) * behind] + [origin + a for a in after[:-1]]
            for r in range(rows):
                for n in range(steps):
                    start = r * block + n * cols
                    u_scr[start:start + cols, :] = before[n][r].astype(BF16).astype(F32)
            send_halo(sweep + 1)
            own_rows()

    for sweep in range(ITERS):
        for side, there in ((0, has_low), (1, has_high)):
            @pl.when(there)
            def _():
                halo_copy(sweep, side).wait_send()
        for k in range(1, n_tm):
            @pl.when(k > z)
            def _():
                t_copy(sweep, k).wait_send()
        s_copy(sweep).wait_send()
    @pl.when((sub == 0) | next_z)
    def _():
        d_copy({"sub": 1 - sub}).wait_send()


def shards(n_chan, n_tm, start_state, guess, w_in, w_mid, w_out, time_embed, levels, plan, offset):
    steps, rows, merged = guess.shape
    ch = w_out.shape[1]
    hid = w_in.shape[1]
    cols = merged // ch
    block = steps * cols
    two = n_chan == 2
    cfg = (steps, rows, cols, ch, hid, n_chan, n_tm, levels.shape[0], plan.shape[0], two)
    n_in = rows + 4 if two else rows + 6
    n_x2 = n_in - 1 if two else n_in - 2
    n_x3 = n_in - 2 if two else n_in - 4
    vmem = pl.BlockSpec(memory_space=pltpu.VMEM)
    smem = pl.BlockSpec(memory_space=pltpu.SMEM)
    anyw = pl.BlockSpec(memory_space=pl.ANY)
    dma = pltpu.SemaphoreType.DMA
    half = rows * cols // 2
    out = pl.pallas_call(
        functools.partial(body, cfg),
        out_shape=jax.ShapeDtypeStruct((steps * rows, merged), F32),
        in_specs=[vmem, vmem, smem, smem, smem, anyw, anyw, anyw, anyw],
        out_specs=vmem,
        scratch_shapes=[
            pltpu.VMEM(w_in.shape, BF16),
            pltpu.VMEM(w_mid.shape, BF16),
            pltpu.VMEM(w_out.shape, BF16),
            pltpu.VMEM(time_embed.shape, BF16),
            pltpu.VMEM((3 * hid, 3 * ch), BF16),
            pltpu.VMEM((n_in * block, 3 * ch), BF16),
            pltpu.VMEM((n_x2 * block, 3 * hid), BF16),
            pltpu.VMEM((n_x3 * block, 3 * hid), BF16),
            pltpu.VMEM((rows * block, ch), F32),
            pltpu.VMEM((rows * cols, ch), F32),
            pltpu.VMEM((rows * block, ch), F32),
            pltpu.VMEM((half, 2 * ch), F32),
            pltpu.VMEM((ITERS, 2, 3 * block // 2, 2 * ch), BF16),
            pltpu.VMEM((ITERS, 2, 3 * block // 2, 2 * ch), BF16),
            pltpu.VMEM((ITERS, half, 2 * ch), F32),
            pltpu.VMEM((ITERS, n_tm, half, 2 * ch), F32),
            pltpu.VMEM((ITERS, half, 2 * ch), F32),
            pltpu.VMEM((ITERS, half, 2 * ch), F32),
            pltpu.VMEM((half, 2 * ch), F32),
            pltpu.VMEM((half, 2 * ch), F32),
            dma((4,)),
            dma((ITERS, 2)),
            dma((ITERS, 2)),
            dma((ITERS, n_tm)),
            dma((ITERS, n_tm)),
            dma((ITERS,)),
            dma((ITERS,)),
            dma,
            dma,
        ],
        compiler_params=pltpu.CompilerParams(
            collective_id=0, has_side_effects=True, vmem_limit_bytes=40 * 1024 * 1024
        ),
    )(start_state, guess, levels, plan, offset, w_in, w_mid, w_out, time_embed)
    return out.reshape(guess.shape)


def solution(mesh):
    return jax.shard_map(
        functools.partial(shards, mesh.shape["chan"], mesh.shape["tm"]),
        mesh=mesh,
        in_specs=(
            P(("parts", "chan"), None),
            P(("parts", "tm", "sub"), "chan", None),
            P(),
            P(),
            P(),
            P(),
            P(),
            P("parts"),
            P("parts"),
        ),
        out_specs=P(("parts", "tm", "sub"), "chan", None),
        check_vma=False,
    )
```

time: 131 us -> 42.8 us (0.33)
  the two profiles are of different devices: /device:TPU:0 before, /device:TPU:25 now
where the time goes in v1:
time: 42.8 us; the launch traced here: 42.3 us
  Pallas kernels  29.7 us (69%)
  local copies, waits for them, and re-layouts  11.8 us (28%)
  between operations  0.76 us (2%)
    pallas_call x1, Pallas kernels, shards(): pl.pallas_call(functools.partial(body, cfg), out_shape=jax.ShapeDtypeStru...  29.7 us
    unnamed x16, local copies, waits for them, and re-layouts  11.1 us

profile of v1, /device:TPU:25, one launch (start us, length us, event | category | flops | bytes accessed | tf_op | source)
XLA Modules:
  0.0 42.3 jit_solution(13203932719328531145)
XLA Ops:
  0.0 0.0 copy-start.5
  0.7 1.2 %copy.10.w_in_hbm = bf16[576,320]{1,0:T(8,128)(2,1)S(1)} copy(bf16[576,320]{0,1:T(8,128)(2,1)} %param.11) | data formatting | bytes 737280 | tf_op args[2]
  2.0 2.2 %copy.12.w_out_hbm = bf16[2880,64]{1,0:T(8,128)(2,1)} copy(bf16[2880,64]{0,1:T(8,128)(2,1)} %param.13) | data formatting | bytes 737280 | tf_op args[4]
  4.1 0.0 copy-done.5
  4.1 0.4 copy.13.te_hbm
  4.5 3.3 %copy.11.w_mid_hbm = bf16[2880,320]{1,0:T(8,128)(2,1)S(1)} copy(bf16[2880,320]{0,1:T(8,128)(2,1)} %param.12) | data formatting | bytes 3686400 | tf_op args[3]
  7.8 0.0 copy-start
  7.8 1.1 %copy-done = bf16[2880,64]{1,0:T(8,128)(2,1)S(1)} copy-done((bf16[2880,64]{1,0:T(8,128)(2,1)S(1)}, bf16[2880,64]{1,0:T(8,128)(2,1)}, u32[]{:S(2)}) %copy-start) | copy-done | bytes 368664
  8.9 0.0 copy-start.1
  8.9 0.8 %copy-done.1 = bf16[4,4,2048]{2,1,0:T(4,128)(2,1)S(1)} copy-done((bf16[4,4,2048]{2,1,0:T(4,128)(2,1)S(1)}, bf16[4,4,2048]{2,1,0:T(4,128)(2,1)}, u32[]{:S(2)}) %copy-start.1) | copy-done | bytes 65560
  9.8 0.0 copy-start.2
  9.8 0.8 %copy-done.2 = f32[4,2048]{1,0:T(4,128)S(1)} copy-done((f32[4,2048]{1,0:T(4,128)S(1)}, f32[4,2048]{1,0:T(4,128)}, u32[]{:S(2)}) %copy-start.2) | copy-done | bytes 32792
  10.5 0.0 copy-start.3
  10.5 0.7 %copy-done.3 = f32[1000]{0:T(1024)S(1)} copy-done((f32[1000]{0:T(1024)S(1)}, f32[1000]{0:T(1024)}, u32[]{:S(2)}) %copy-start.3) | copy-done | bytes 4024
  11.2 0.0 copy-start.4
  11.2 0.7 %copy-done.4 = s32[65]{0:T(128)S(1)} copy-done((s32[65]{0:T(128)S(1)}, s32[65]{0:T(128)}, u32[]{:S(2)}) %copy-start.4) | copy-done | bytes 284
  11.9 29.7 %shard_map.91 = f32[16,2048]{1,0:T(8,128)S(1)} custom-call(f32[4,2048]{1,0:T(4,128)S(1)} %copy-done.2, bf16[4,4,2048]{2,1,0:T(4,128)(2,1)S(1)} %copy-done.1, f32[1000]{0:T(1024)S(1)} %copy-done.3, s32[65]{0:T(128)S(1)} %copy-done.4, s32[1]{0:T(128)S(6)} %copy.14.offset_ref, bf16[576,320]{1,0:T(8,128)(2,1)S(1)} %copy.10.w_in_hbm, ...), custom_call_target="tpu_custom_call" | custom-call | tf_op jit(solution)/shard_map/pallas_call | solution.py:321
  41.6 0.7 %reshape.3 = f32[4,4,2048]{2,1,0:T(4,128)} reshape(f32[16,2048]{1,0:T(8,128)S(1)} %shard_map.91) | data formatting | bytes 262144 | tf_op jit(solution)/shard_map/reshape | solution.py:361
Async XLA Ops:
  0.0 4.1 %copy-start.5 = (bf16[1000,320]{0,1:T(8,128)(2,1)S(1)}, bf16[1000,320]{0,1:T(8,128)(2,1)}, u32[]{:S(2)}) copy-start(bf16[1000,320]{0,1:T(8,128)(2,1)} %param.14) | copy-start | bytes 1920004
  7.8 1.1 %copy-start = (bf16[2880,64]{1,0:T(8,128)(2,1)S(1)}, bf16[2880,64]{1,0:T(8,128)(2,1)}, u32[]{:S(2)}) copy-start(bf16[2880,64]{1,0:T(8,128)(2,1)} %copy.12.w_out_hbm) | copy-start | bytes 1105924
  8.9 0.8 %copy-start.1 = (bf16[4,4,2048]{2,1,0:T(4,128)(2,1)S(1)}, bf16[4,4,2048]{2,1,0:T(4,128)(2,1)}, u32[]{:S(2)}) copy-start(bf16[4,4,2048]{2,1,0:T(4,128)(2,1)} %guess_ref.1) | copy-start | bytes 196612
  9.8 0.8 %copy-start.2 = (f32[4,2048]{1,0:T(4,128)S(1)}, f32[4,2048]{1,0:T(4,128)}, u32[]{:S(2)}) copy-start(f32[4,2048]{1,0:T(4,128)} %start_ref.1) | copy-start | bytes 98308
  10.5 0.7 %copy-start.3 = (f32[1000]{0:T(1024)S(1)}, f32[1000]{0:T(1024)}, u32[]{:S(2)}) copy-start(f32[1000]{0:T(1024)} %levels_ref.1) | copy-start | bytes 12004
  11.2 0.7 %copy-start.4 = (s32[65]{0:T(128)S(1)}, s32[65]{0:T(128)}, u32[]{:S(2)}) copy-start(s32[65]{0:T(128)} %plan_ref.1) | copy-start | bytes 784

commit v2 on v1

--- a/solution.py
+++ b/solution.py
@@ -18,6 +18,10 @@
     return half + half * jnp.tanh(half)
 
 
+def dot(left, right):
+    return lax.dot_general(left, right, (((1,), (1,)), ((), ())), preferred_element_type=F32)
+
+
 def fold(array):
     half = array.shape[0] // 2
     return jnp.concatenate([array[:half], array[half:]], axis=1)
@@ -30,9 +34,10 @@
 
 def body(
     cfg,
-    start_ref, guess_ref, levels_ref, plan_ref, offset_ref, w_in_hbm, w_mid_hbm, w_out_hbm, te_hbm,
+    start_hbm, guess_hbm, levels_hbm, plan_hbm, offset_hbm, w_in_hbm, w_mid_hbm, w_out_hbm, te_hbm,
     out_ref,
-    w_in, w_mid, w_out, te, w_sum, x1, x2, x3, u_scr, st_scr, o_scr, p_scr,
+    start_ref, guess_ref, levels_ref, plan_ref, offset_ref,
+    w_in_raw, w_mid_raw, w_out_raw, te, w_in, w_mid, w_sum, x1, x2, x3, u_scr, st_scr, o_scr, p_scr,
     halo_send, halo_recv, t_send, t_recv, s_send, s_recv, d_send, d_recv,
     w_sem, hs_sem, hr_sem, ts_sem, tr_sem, ss_sem, sr_sem, ds_sem, dr_sem,
 ):
@@ -48,7 +53,11 @@
     weights = [
         pltpu.make_async_copy(src, dst, w_sem.at[i])
         for i, (src, dst) in enumerate(
-            [(w_in_hbm, w_in), (te_hbm, te), (w_mid_hbm, w_mid), (w_out_hbm, w_out)]
+            [
+                (guess_hbm, guess_ref), (start_hbm, start_ref), (levels_hbm, levels_ref),
+                (plan_hbm, plan_ref), (offset_hbm, offset_ref), (w_in_hbm, w_in_raw),
+                (te_hbm, te), (w_mid_hbm, w_mid_raw), (w_out_hbm, w_out_raw),
+            ]
         )
     ]
     for copy in weights:
@@ -79,10 +88,12 @@
     def _():
         hello({"chan": chan + 1})
 
+    weights[0].wait()
     for n in range(steps):
         tile = guess_ref[n].astype(F32)
         for c in range(cols):
             u_scr[pl.ds(n * cols + c, rows, stride=block), :] = tile[:, c * ch:(c + 1) * ch]
+    weights[1].wait()
     for c in range(cols):
         st_scr[pl.ds(c, rows, stride=cols), :] = start_ref[:, c * ch:(c + 1) * ch]
 
@@ -149,6 +160,8 @@
 
     send_halo(0)
 
+    for i in (2, 3, 4):
+        weights[i].wait()
     base = offset_ref[0] + first
     ids = [plan_ref[jnp.minimum(base + n, n_plan - 1)] for n in range(steps + 2)]
     noise = [levels_ref[i] for i in ids]
@@ -177,14 +190,16 @@
             x1[at(own + r), :] = spread(u_scr[r * block:(r + 1) * block, :])
 
     own_rows()
-    weights[0].wait()
-    weights[1].wait()
+    weights[5].wait()
+    for kr in range(3):
+        w_in[kr] = w_in_raw[:, kr * 3 * ch:(kr + 1) * 3 * ch]
+    weights[6].wait()
     hot = jnp.zeros((8, n_levels), F32)
     row_of = lax.broadcasted_iota(jnp.int32, (8, n_levels), 0)
     id_of = lax.broadcasted_iota(jnp.int32, (8, n_levels), 1)
     for n in range(steps):
         hot = jnp.where((row_of == n) & (id_of == ids[n]), 1.0, hot)
-    embed8 = jnp.dot(hot.astype(BF16), te[...], preferred_element_type=F32)
+    embed8 = dot(hot.astype(BF16), te[...])
     embed = jnp.concatenate(
         [jnp.broadcast_to(embed8[n:n + 1], (cols, hid)) for n in range(steps)], axis=0
     )
@@ -197,35 +212,31 @@
                 got = unfold(halo_recv[sweep, side].astype(F32))
                 for r in range(3):
                     x1[at(r if side == 1 else own + rows + r), :] = spread(got[r * block:(r + 1) * block])
-        act = jnp.dot(x1[0:n1 * block, :], w_in[0:3 * ch, :], preferred_element_type=F32)
+        act = dot(x1[0:n1 * block, :], w_in[0])
         for kr in (1, 2):
-            act += jnp.dot(
-                x1[kr * block:(kr + n1) * block, :], w_in[kr * 3 * ch:(kr + 1) * 3 * ch, :],
-                preferred_element_type=F32,
-            )
+            act += dot(x1[kr * block:(kr + n1) * block, :], w_in[kr])
         for r in range(n1):
             hidden = silu(act[r * block:(r + 1) * block] + embed)
             if not two:
                 hidden = hidden * chosen(n1, -2, r)
             x2[at(o1 + r), :] = spread(hidden)
         if sweep == 0:
-            weights[2].wait()
-        act = jnp.dot(x2[0:n2 * block, :], w_mid[0:3 * hid, :], preferred_element_type=F32)
+            weights[7].wait()
+            for kr in range(3):
+                w_mid[kr] = w_mid_raw[:, kr * 3 * hid:(kr + 1) * 3 * hid]
+        act = dot(x2[0:n2 * block, :], w_mid[0])
         for kr in (1, 2):
-            act += jnp.dot(
-                x2[kr * block:(kr + n2) * block, :], w_mid[kr * 3 * hid:(kr + 1) * 3 * hid, :],
-                preferred_element_type=F32,
-            )
+            act += dot(x2[kr * block:(kr + n2) * block, :], w_mid[kr])
         for r in range(n2):
             hidden = silu(act[r * block:(r + 1) * block])
             if not two:
                 hidden = hidden * chosen(n2, -1, r)
             x3[at(o1 + r), :] = spread(hidden)
         if sweep == 0:
-            weights[3].wait()
+            weights[8].wait()
             for kr in range(3):
-                w_sum[:, kr * ch:(kr + 1) * ch] = w_out[kr * 3 * hid:(kr + 1) * 3 * hid, :]
-        taps = jnp.dot(x3[...], w_sum[...], preferred_element_type=F32)
+                w_sum[kr * ch:(kr + 1) * ch, :] = w_out_raw[:, kr * 3 * hid:(kr + 1) * 3 * hid]
+        taps = dot(x3[...], w_sum[...])
         size_out = rows * block
         drift = (
             taps[0:size_out, 0:ch]
@@ -314,21 +325,27 @@
     n_x2 = n_in - 1 if two else n_in - 2
     n_x3 = n_in - 2 if two else n_in - 4
     vmem = pl.BlockSpec(memory_space=pltpu.VMEM)
-    smem = pl.BlockSpec(memory_space=pltpu.SMEM)
-    anyw = pl.BlockSpec(memory_space=pl.ANY)
+    hbm = pl.BlockSpec(memory_space=pltpu.HBM)
     dma = pltpu.SemaphoreType.DMA
     half = rows * cols // 2
     out = pl.pallas_call(
         functools.partial(body, cfg),
         out_shape=jax.ShapeDtypeStruct((steps * rows, merged), F32),
-        in_specs=[vmem, vmem, smem, smem, smem, anyw, anyw, anyw, anyw],
+        in_specs=[hbm] * 9,
         out_specs=vmem,
         scratch_shapes=[
-            pltpu.VMEM(w_in.shape, BF16),
-            pltpu.VMEM(w_mid.shape, BF16),
-            pltpu.VMEM(w_out.shape, BF16),
-            pltpu.VMEM(time_embed.shape, BF16),
-            pltpu.VMEM((3 * hid, 3 * ch), BF16),
+            pltpu.VMEM(start_state.shape, F32),
+            pltpu.VMEM(guess.shape, BF16),
+            pltpu.SMEM(levels.shape, F32),
+            pltpu.SMEM(plan.shape, jnp.int32),
+            pltpu.SMEM(offset.shape, jnp.int32),
+            pltpu.VMEM(w_in.shape[::-1], BF16),
+            pltpu.VMEM(w_mid.shape[::-1], BF16),
+            pltpu.VMEM(w_out.shape[::-1], BF16),
+            pltpu.VMEM(time_embed.shape[::-1], BF16),
+            pltpu.VMEM((3, hid, 3 * ch), BF16),
+            pltpu.VMEM((3, hid, 3 * hid), BF16),
+            pltpu.VMEM((3 * ch, 3 * hid), BF16),
             pltpu.VMEM((n_in * block, 3 * ch), BF16),
             pltpu.VMEM((n_x2 * block, 3 * hid), BF16),
             pltpu.VMEM((n_x3 * block, 3 * hid), BF16),
@@ -344,7 +361,7 @@
             pltpu.VMEM((ITERS, half, 2 * ch), F32),
             pltpu.VMEM((half, 2 * ch), F32),
             pltpu.VMEM((half, 2 * ch), F32),
-            dma((4,)),
+            dma((9,)),
             dma((ITERS, 2)),
             dma((ITERS, 2)),
             dma((ITERS, n_tm)),
@@ -355,9 +372,9 @@
             dma,
         ],
         compiler_params=pltpu.CompilerParams(
-            collective_id=0, has_side_effects=True, vmem_limit_bytes=40 * 1024 * 1024
+            collective_id=0, has_side_effects=True, vmem_limit_bytes=60 * 1024 * 1024
         ),
-    )(start_state, guess, levels, plan, offset, w_in, w_mid, w_out, time_embed)
+    )(start_state, guess, levels, plan, offset, w_in.T, w_mid.T, w_out.T, time_embed.T)
     return out.reshape(guess.shape)
 
 

time: 42.8 us -> 31.2 us (0.73)
  local copies, waits for them, and re-layouts: 11.8 us -> 1.6 us
  Pallas kernels: 29.7 us -> 28.8 us
    unnamed x16 -> x0, local copies, waits for them, and re-layouts: 11.1 us -> none
    reshape x1, local copies, waits for them, and re-layouts: 0.69 us -> 1.6 us  [shards(): return out.reshape(guess.shape)]
    pallas_call x1, Pallas kernels: 29.7 us -> 28.8 us  [shards(): pl.pallas_call(functools.partial(body, cfg), out_shape=jax.ShapeDtypeStru...]
where the time goes in v2:
time: 31.2 us; the launch traced here: 31.1 us
  Pallas kernels  28.8 us (92%)
  local copies, waits for them, and re-layouts  1.6 us (5%)
  between operations  0.66 us (2%)
    pallas_call x1, Pallas kernels, shards(): pl.pallas_call(functools.partial(body, cfg), out_shape=jax.ShapeDtypeStru...  28.8 us
    reshape x1, local copies, waits for them, and re-layouts, shards(): return out.reshape(guess.shape)  1.6 us

profile of v2, /device:TPU:25, one launch (start us, length us, event | category | flops | bytes accessed | tf_op | source)
XLA Modules:
  0.0 31.1 jit_solution(14987638586016314494)
XLA Ops:
  0.7 28.8 %shard_map.91 = f32[16,2048]{1,0:T(8,128)} custom-call(f32[4,2048]{1,0:T(4,128)} %start_hbm.1, bf16[4,4,2048]{2,1,0:T(4,128)(2,1)} %guess_hbm.1, f32[1000]{0:T(1024)} %levels_hbm.1, s32[65]{0:T(128)} %plan_hbm.1, s32[1]{0:T(128)S(6)} %copy.10.offset_hbm, bf16[320,576]{1,0:T(8,128)(2,1)} %bitcast.6, bf16[320,2880]{1,0:T(8,128)(2,1)} %bitcast.4, ...), custom_call_target="tpu_custom_call" | custom-call | tf_op jit(solution)/shard_map/pallas_call | solution.py:331
  29.5 1.6 %reshape.3 = f32[4,4,2048]{2,1,0:T(4,128)} reshape(f32[16,2048]{1,0:T(8,128)} %shard_map.91) | data formatting | bytes 262144 | tf_op jit(solution)/shard_map/reshape | solution.py:378

commit v3 on v2

--- a/solution.py
+++ b/solution.py
@@ -37,12 +37,13 @@
     start_hbm, guess_hbm, levels_hbm, plan_hbm, offset_hbm, w_in_hbm, w_mid_hbm, w_out_hbm, te_hbm,
     out_ref,
     start_ref, guess_ref, levels_ref, plan_ref, offset_ref,
-    w_in_raw, w_mid_raw, w_out_raw, te, w_in, w_mid, w_sum, x1, x2, x3, u_scr, st_scr, o_scr, p_scr,
+    w_in_raw, w_mid_raw, w_out_raw, te, w_in, w_mid, w_rest, w_sum, x1, x2, x3, u_scr, st_scr, o_scr, p_scr,
     halo_send, halo_recv, t_send, t_recv, s_send, s_recv, d_send, d_recv,
     w_sem, hs_sem, hr_sem, ts_sem, tr_sem, ss_sem, sr_sem, ds_sem, dr_sem,
 ):
     steps, rows, cols, ch, hid, n_chan, n_tm, n_levels, n_plan, two = cfg
     block = steps * cols
+    n_rest = hid % 128
     z = lax.axis_index("tm")
     sub = lax.axis_index("sub")
     chan = lax.axis_index("chan")
@@ -204,6 +205,15 @@
         [jnp.broadcast_to(embed8[n:n + 1], (cols, hid)) for n in range(steps)], axis=0
     )
 
+    weights[7].wait()
+    for kr in range(3):
+        taps_of = slice(kr * 3 * hid, (kr + 1) * 3 * hid)
+        w_mid[kr] = w_mid_raw[0:hid - n_rest, taps_of]
+        w_rest[kr * n_rest:(kr + 1) * n_rest, :] = w_mid_raw[hid - n_rest:hid, taps_of]
+    weights[8].wait()
+    for kr in range(3):
+        w_sum[kr * ch:(kr + 1) * ch, :] = w_out_raw[:, kr * 3 * hid:(kr + 1) * 3 * hid]
+
     for sweep in range(ITERS):
         for side, there in ((1, has_low), (0, has_high)):
             @pl.when(there)
@@ -220,22 +230,19 @@
             if not two:
                 hidden = hidden * chosen(n1, -2, r)
             x2[at(o1 + r), :] = spread(hidden)
-        if sweep == 0:
-            weights[7].wait()
-            for kr in range(3):
-                w_mid[kr] = w_mid_raw[:, kr * 3 * hid:(kr + 1) * 3 * hid]
-        act = dot(x2[0:n2 * block, :], w_mid[0])
+        main = dot(x2[0:n2 * block, :], w_mid[0])
         for kr in (1, 2):
-            act += dot(x2[kr * block:(kr + n2) * block, :], w_mid[kr])
+            main += dot(x2[kr * block:(kr + n2) * block, :], w_mid[kr])
+        rest = dot(x2[0:(n2 + 2) * block, :], w_rest[...])
         for r in range(n2):
-            hidden = silu(act[r * block:(r + 1) * block])
+            tail = sum(
+                rest[(r + kr) * block:(r + kr + 1) * block, kr * n_rest:(kr + 1) * n_rest]
+                for kr in range(3)
+            )
+            hidden = silu(jnp.concatenate([main[r * block:(r + 1) * block], tail], axis=1))
             if not two:
                 hidden = hidden * chosen(n2, -1, r)
             x3[at(o1 + r), :] = spread(hidden)
-        if sweep == 0:
-            weights[8].wait()
-            for kr in range(3):
-                w_sum[kr * ch:(kr + 1) * ch, :] = w_out_raw[:, kr * 3 * hid:(kr + 1) * 3 * hid]
         taps = dot(x3[...], w_sum[...])
         size_out = rows * block
         drift = (
@@ -251,13 +258,13 @@
             total = total + onward[n] * drift[:, n]
         last = sweep == ITERS - 1
         total = fold(total.reshape(rows * cols, ch))
-        t_send[sweep] = total
+        t_send[sweep] = total.astype(BF16)
         for k in range(1, n_tm):
             @pl.when(k > z)
             def _():
                 t_copy(sweep, k).start()
         if not last:
-            d_send[...] = fold(drift[:, steps - 1].reshape(rows * cols, ch))
+            d_send[...] = fold(drift[:, steps - 1].reshape(rows * cols, ch)).astype(BF16)
             @pl.when(sub == 0)
             def _():
                 d_copy({"sub": 1}).start()
@@ -269,7 +276,7 @@
             @pl.when(k < z)
             def _():
                 t_arrived(sweep, k).wait_recv()
-                p_scr[...] += t_recv[sweep, k]
+                p_scr[...] += t_recv[sweep, k].astype(F32)
         s_send[sweep] = p_scr[...] + jnp.where(sub == 0, total, 0.0)
         s_copy(sweep).start()
         s_copy(sweep).wait_recv()
@@ -280,15 +287,17 @@
             for n in range(steps):
                 o_scr[n * rows * cols:(n + 1) * rows * cols, :] = (origin + after[n]).reshape(rows * cols, ch)
             for c in range(0, cols, 2):
-                out_ref[:, c * ch:(c + 2) * ch] = jnp.concatenate(
+                pair = jnp.concatenate(
                     [o_scr[pl.ds(c + i, steps * rows, stride=cols), :] for i in range(2)], axis=1
                 )
+                for n in range(steps):
+                    out_ref[n, :, c * ch:(c + 2) * ch] = pair[n * rows:(n + 1) * rows]
         else:
             p_scr[...] = jnp.zeros(p_scr.shape, F32)
             @pl.when((sub == 1) | prev_z)
             def _():
                 d_copy({"sub": 1 - sub}).wait_recv()
-                p_scr[...] = d_recv[...]
+                p_scr[...] = d_recv[...].astype(F32)
             behind = unfold(p_scr[...]).reshape(rows, cols, ch)
             before = [origin + (0.5 * size[0]) * behind] + [origin + a for a in after[:-1]]
             for r in range(rows):
@@ -330,7 +339,7 @@
     half = rows * cols // 2
     out = pl.pallas_call(
         functools.partial(body, cfg),
-        out_shape=jax.ShapeDtypeStruct((steps * rows, merged), F32),
+        out_shape=jax.ShapeDtypeStruct(guess.shape, F32),
         in_specs=[hbm] * 9,
         out_specs=vmem,
         scratch_shapes=[
@@ -344,7 +353,8 @@
             pltpu.VMEM(w_out.shape[::-1], BF16),
             pltpu.VMEM(time_embed.shape[::-1], BF16),
             pltpu.VMEM((3, hid, 3 * ch), BF16),
-            pltpu.VMEM((3, hid, 3 * hid), BF16),
+            pltpu.VMEM((3, hid - hid % 128, 3 * hid), BF16),
+            pltpu.VMEM((3 * (hid % 128), 3 * hid), BF16),
             pltpu.VMEM((3 * ch, 3 * hid), BF16),
             pltpu.VMEM((n_in * block, 3 * ch), BF16),
             pltpu.VMEM((n_x2 * block, 3 * hid), BF16),
@@ -355,12 +365,12 @@
             pltpu.VMEM((half, 2 * ch), F32),
             pltpu.VMEM((ITERS, 2, 3 * block // 2, 2 * ch), BF16),
             pltpu.VMEM((ITERS, 2, 3 * block // 2, 2 * ch), BF16),
-            pltpu.VMEM((ITERS, half, 2 * ch), F32),
-            pltpu.VMEM((ITERS, n_tm, half, 2 * ch), F32),
+            pltpu.VMEM((ITERS, half, 2 * ch), BF16),
+            pltpu.VMEM((ITERS, n_tm, half, 2 * ch), BF16),
             pltpu.VMEM((ITERS, half, 2 * ch), F32),
             pltpu.VMEM((ITERS, half, 2 * ch), F32),
-            pltpu.VMEM((half, 2 * ch), F32),
-            pltpu.VMEM((half, 2 * ch), F32),
+            pltpu.VMEM((half, 2 * ch), BF16),
+            pltpu.VMEM((half, 2 * ch), BF16),
             dma((9,)),
             dma((ITERS, 2)),
             dma((ITERS, 2)),
@@ -375,7 +385,7 @@
             collective_id=0, has_side_effects=True, vmem_limit_bytes=60 * 1024 * 1024
         ),
     )(start_state, guess, levels, plan, offset, w_in.T, w_mid.T, w_out.T, time_embed.T)
-    return out.reshape(guess.shape)
+    return out
 
 
 def solution(mesh):

time: 31.2 us -> 29.4 us (0.942)
  Pallas kernels: 28.8 us -> 27 us
    pallas_call x1, Pallas kernels: 28.8 us -> 27 us  [shards(): pl.pallas_call(functools.partial(body, cfg), out_shape=jax.ShapeDtypeStru...]
    reshape x1 -> x0, local copies, waits for them, and re-layouts: 1.6 us -> none  [shards(): return out.reshape(guess.shape)]
    unnamed x0 -> x1, local copies, waits for them, and re-layouts: none -> 1.57 us
where the time goes in v3:
time: 29.4 us; the launch traced here: 29.2 us
  Pallas kernels  27 us (92%)
  local copies, waits for them, and re-layouts  1.57 us (5%)
  between operations  0.66 us (2%)
    pallas_call x1, Pallas kernels, shards(): pl.pallas_call(functools.partial(body, cfg), out_shape=jax.ShapeDtypeStru...  27 us
    unnamed x1, local copies, waits for them, and re-layouts  1.57 us

profile of v3, /device:TPU:25, one launch (start us, length us, event | category | flops | bytes accessed | tf_op | source)
XLA Modules:
  0.0 29.2 jit_solution(16750520930504842245)
XLA Ops:
  0.7 27.0 %shard_map.91 = f32[4,4,2048]{2,1,0:T(4,128)} custom-call(f32[4,2048]{1,0:T(4,128)} %start_hbm.1, bf16[4,4,2048]{2,1,0:T(4,128)(2,1)} %guess_hbm.1, f32[1000]{0:T(1024)} %levels_hbm.1, s32[65]{0:T(128)} %plan_hbm.1, s32[1]{0:T(128)S(6)} %copy.11.offset_hbm, bf16[320,576]{1,0:T(8,128)(2,1)} %bitcast.6, bf16[320,2880]{1,0:T(8,128)(2,1)} %bitcast.4, ...), custom_call_target="tpu_custom_call" | custom-call | tf_op jit(solution)/shard_map/pallas_call | solution.py:340
  27.7 1.6 %copy.12 = f32[4,4,2048]{2,1,0:T(4,128)} copy(f32[4,4,2048]{2,1,0:T(4,128)} %shard_map.91) | data formatting | bytes 262144

commit v4 on v3

--- a/solution.py
+++ b/solution.py
@@ -214,7 +214,20 @@
     for kr in range(3):
         w_sum[kr * ch:(kr + 1) * ch, :] = w_out_raw[:, kr * 3 * hid:(kr + 1) * 3 * hid]
 
+    def first_layer(start, count):
+        def taps(kr):
+            return x1[pl.ds((start + kr) * block if isinstance(start, int) else pl.multiple_of((start + kr) * block, block), count * block), :]
+
+        act = dot(taps(0), w_in[0]) + dot(taps(1), w_in[1]) + dot(taps(2), w_in[2])
+        for r in range(count):
+            hidden = silu(act[r * block:(r + 1) * block] + embed)
+            if not two:
+                hidden = hidden * chosen(n1, -2, r)
+            x2[at(o1 + start + r), :] = spread(hidden)
+
     for sweep in range(ITERS):
+        if two:
+            first_layer(3 * chan, n1 // 2)
         for side, there in ((1, has_low), (0, has_high)):
             @pl.when(there)
             def _():
@@ -222,14 +235,7 @@
                 got = unfold(halo_recv[sweep, side].astype(F32))
                 for r in range(3):
                     x1[at(r if side == 1 else own + rows + r), :] = spread(got[r * block:(r + 1) * block])
-        act = dot(x1[0:n1 * block, :], w_in[0])
-        for kr in (1, 2):
-            act += dot(x1[kr * block:(kr + n1) * block, :], w_in[kr])
-        for r in range(n1):
-            hidden = silu(act[r * block:(r + 1) * block] + embed)
-            if not two:
-                hidden = hidden * chosen(n1, -2, r)
-            x2[at(o1 + r), :] = spread(hidden)
+        first_layer(3 * (1 - chan) if two else 0, n1 // 2 if two else n1)
         main = dot(x2[0:n2 * block, :], w_mid[0])
         for kr in (1, 2):
             main += dot(x2[kr * block:(kr + n2) * block, :], w_mid[kr])
@@ -259,7 +265,7 @@
         last = sweep == ITERS - 1
         total = fold(total.reshape(rows * cols, ch))
         t_send[sweep] = total.astype(BF16)
-        for k in range(1, n_tm):
+        for k in range(n_tm - 1, 0, -1):
             @pl.when(k > z)
             def _():
                 t_copy(sweep, k).start()
@@ -328,7 +334,7 @@
     hid = w_in.shape[1]
     cols = merged // ch
     block = steps * cols
-    two = n_chan == 2
+    two = n_chan == 2 and rows == 4
     cfg = (steps, rows, cols, ch, hid, n_chan, n_tm, levels.shape[0], plan.shape[0], two)
     n_in = rows + 4 if two else rows + 6
     n_x2 = n_in - 1 if two else n_in - 2

time: 29.4 us -> 28.6 us (0.973)
  Pallas kernels: 27 us -> 25.9 us
    pallas_call x1, Pallas kernels: 27 us -> 25.9 us  [shards(): pl.pallas_call(functools.partial(body, cfg), out_shape=jax.ShapeDtypeStru...]
where the time goes in v4:
time: 28.6 us; the launch traced here: 28.2 us
  Pallas kernels  25.9 us (91%)
  local copies, waits for them, and re-layouts  1.57 us (5%)
  between operations  0.66 us (2%)
    pallas_call x1, Pallas kernels, shards(): pl.pallas_call(functools.partial(body, cfg), out_shape=jax.ShapeDtypeStru...  25.9 us
    unnamed x1, local copies, waits for them, and re-layouts  1.57 us

profile of v4, /device:TPU:25, one launch (start us, length us, event | category | flops | bytes accessed | tf_op | source)
XLA Modules:
  0.0 28.2 jit_solution(8133224581936487449)
XLA Ops:
  0.7 25.9 %shard_map.91 = f32[4,4,2048]{2,1,0:T(4,128)} custom-call(f32[4,2048]{1,0:T(4,128)} %start_hbm.1, bf16[4,4,2048]{2,1,0:T(4,128)(2,1)} %guess_hbm.1, f32[1000]{0:T(1024)} %levels_hbm.1, s32[65]{0:T(128)} %plan_hbm.1, s32[1]{0:T(128)S(6)} %copy.11.offset_hbm, bf16[320,576]{1,0:T(8,128)(2,1)} %bitcast.6, bf16[320,2880]{1,0:T(8,128)(2,1)} %bitcast.4, ...), custom_call_target="tpu_custom_call" | custom-call | tf_op jit(solution)/shard_map/pallas_call | solution.py:346
  26.6 1.6 %copy.12 = f32[4,4,2048]{2,1,0:T(4,128)} copy(f32[4,4,2048]{2,1,0:T(4,128)} %shard_map.91) | data formatting | bytes 262144

commit v5 on v4

--- a/solution.py
+++ b/solution.py
@@ -258,9 +258,7 @@
         ).reshape(rows, steps, cols, ch)
 
         total = jnp.zeros((rows, cols, ch), F32)
-        after = []
         for n in range(steps):
-            after.append(total + front[n] * drift[:, n])
             total = total + onward[n] * drift[:, n]
         last = sweep == ITERS - 1
         total = fold(total.reshape(rows * cols, ch))
@@ -277,6 +275,11 @@
             @pl.when(next_z)
             def _():
                 d_copy({"tm": z + 1, "sub": 0}).start()
+        running = jnp.zeros((rows, cols, ch), F32)
+        after = []
+        for n in range(steps):
+            after.append(running + front[n] * drift[:, n])
+            running = running + onward[n] * drift[:, n]
         p_scr[...] = jnp.zeros(p_scr.shape, F32)
         for k in range(n_tm - 1):
             @pl.when(k < z)

time: 28.6 us -> 28.6 us (level)
  no operation moved by 1% of the time
where the time goes in v5:
time: 28.6 us; the launch traced here: 28.2 us
  Pallas kernels  25.9 us (91%)
  local copies, waits for them, and re-layouts  1.57 us (5%)
  between operations  0.66 us (2%)
    pallas_call x1, Pallas kernels, shards(): pl.pallas_call(functools.partial(body, cfg), out_shape=jax.ShapeDtypeStru...  25.9 us
    unnamed x1, local copies, waits for them, and re-layouts  1.57 us

profile of v5, /device:TPU:25, one launch (start us, length us, event | category | flops | bytes accessed | tf_op | source)
XLA Modules:
  0.0 28.2 jit_solution(6154734396819663367)
XLA Ops:
  0.7 25.9 %shard_map.91 = f32[4,4,2048]{2,1,0:T(4,128)} custom-call(f32[4,2048]{1,0:T(4,128)} %start_hbm.1, bf16[4,4,2048]{2,1,0:T(4,128)(2,1)} %guess_hbm.1, f32[1000]{0:T(1024)} %levels_hbm.1, s32[65]{0:T(128)} %plan_hbm.1, s32[1]{0:T(128)S(6)} %copy.11.offset_hbm, bf16[320,576]{1,0:T(8,128)(2,1)} %bitcast.6, bf16[320,2880]{1,0:T(8,128)(2,1)} %bitcast.4, ...), custom_call_target="tpu_custom_call" | custom-call | tf_op jit(solution)/shard_map/pallas_call | solution.py:349
  26.6 1.6 %copy.12 = f32[4,4,2048]{2,1,0:T(4,128)} copy(f32[4,4,2048]{2,1,0:T(4,128)} %shard_map.91) | data formatting | bytes 262144
